TPU v7x, 32 devices: a whole 2x2x4 slice. The times are simulated.
32 devices in a mesh: blk: 16 (over z, x, core), src: 2 (over y).
Axes of the slice: x: 2, y: 2, z: 4, core: 2. Of those that a mesh axis runs over, the one named last changes fastest.
Arguments:
- raw_records: float32 [512, 10240], P('blk', 'src'), may hold values from -6 to 6
- fir_taps: float32 [64], replicated, may hold values from -0.75 to 0.75
- alive_mask: int32 [512], P('blk'), may hold values 0 or 1
- source_index: int32 [16, 2], P('blk'), may hold values from 0 to 31
Outputs:
- correlations: bfloat16 [32, 512, 512], P('src', 'blk')
All inputs are finite; a program needn't handle non-finite values. No bound on the sum of `alive_mask` on one device may be relied on, other than what follows from the above.
Results may differ from a plain program's by a relative error of at most 0.0053.
Values sent between devices are 32-bit elements; how exact they have to be, the bound alone decides.
No kernel may reach another device: no remote copies, remote signals or barrier semaphores. Data moves between devices by JAX's collectives and lax.ppermute only.
A program may use at most 128 MiB of HBM per device.

v0:
```python
import math

import jax
import jax.numpy as jnp
import numpy as np
from jax import lax
from jax.experimental import pallas as pl
from jax.experimental.pallas import tpu as pltpu
from jax.sharding import PartitionSpec as P

S = 512
NFFT = 1024
BINS = NFFT // 2
LAGS = 512
TAPS = 64
DEC = 20
HALF = 64
LANES = 128
SUBLANES = 8
PARTS = 3
EDGE = (TAPS - 1) // DEC
CHUNK = 640
CHUNK_OUT = CHUNK // DEC
VMEM_LIMIT = 48 * 1024 * 1024


def forward_table():
    phases = 2.0 * math.pi / NFFT * (np.outer(np.arange(S // 2), np.arange(BINS)) % NFFT)
    return np.concatenate([np.cos(phases), -np.sin(phases)], axis=1).astype(np.float32)


def split_table(table):
    high = table.astype(jnp.bfloat16)
    low = (table - high.astype(np.float32)).astype(jnp.bfloat16)
    return high, low


def band_table():
    bins = np.arange(3 * LANES)[:, None] - LANES
    return (np.abs(bins - np.arange(LANES)[None, :]) <= HALF).astype(jnp.bfloat16)


def lag_table():
    bins = np.arange(BINS)[:, None]
    shift = np.arange(LAGS)[None, :] - LAGS // 2
    phases = 2.0 * math.pi / NFFT * (bins * shift % NFFT)
    weight = np.where(bins == 0, 0.5, 1.0) / math.sqrt(BINS)
    table = np.concatenate([weight * np.cos(phases), -weight * np.sin(phases)], axis=0)
    return table.astype(np.float32).astype(jnp.bfloat16)


def split(value):
    high = value.astype(jnp.bfloat16)
    return high, (value - high.astype(jnp.float32)).astype(jnp.bfloat16)


def dot(a, b):
    return jnp.dot(a, b, preferred_element_type=jnp.float32)


def column(row):
    count = row.shape[1]
    at = [lax.broadcasted_iota(jnp.int32, (count, count), axis) for axis in range(2)]
    rows = jnp.broadcast_to(row, (count, count))
    return jnp.sum(jnp.where(at[0] == at[1], rows, 0.0), axis=1, keepdims=True)


def start_copies(pairs, sems):
    copies = [
        pltpu.make_async_copy(source, target, sems.at[at])
        for at, (source, target) in enumerate(pairs)
    ]
    for copy in copies:
        copy.start()
    return copies


def decimate_kernel(
    paired, raw_hbm, taps_hbm, alive_hbm, picks_hbm, out_ref, pieces_hbm,
    raw_ref, taps_ref, alive_ref, picks_ref, source_ref, pieces_ref, sems,
):
    rows = raw_hbm.shape[0]
    chunks = raw_hbm.shape[1] // CHUNK
    slots = picks_ref.shape[1]
    per_tile = LANES // CHUNK_OUT
    tiles = -(-chunks // per_tile)
    pairs = [(taps_hbm, taps_ref), (picks_hbm, picks_ref), (alive_hbm, alive_ref)]
    for at in range(0, rows, SUBLANES):
        span = slice(at, at + SUBLANES)
        pairs.append((raw_hbm.at[span], raw_ref.at[span]))
    copies = start_copies(pairs, sems)
    source_ref[...] = jnp.zeros_like(source_ref)
    copies[0].wait()
    taps = jnp.broadcast_to(taps_ref[...], (SUBLANES, TAPS))
    eight = jnp.concatenate([taps, jnp.zeros((SUBLANES, CHUNK - TAPS), jnp.float32)], axis=1)
    for _ in range(2):
        eight = pltpu.roll(eight, 0, 1, stride=DEC // 2, stride_axis=0)
    wrapped = jnp.concatenate(
        [eight]
        + [pltpu.roll(eight, DEC * at, 1) for at in range(SUBLANES, CHUNK_OUT, SUBLANES)],
        axis=0,
    )
    lane = lax.broadcasted_iota(jnp.int32, (CHUNK_OUT, CHUNK), 1)
    row = lax.broadcasted_iota(jnp.int32, (CHUNK_OUT, CHUNK), 0)
    main = jnp.where(lane >= DEC * row, wrapped, 0.0)
    rim = wrapped - main
    gap = jnp.zeros((LANES - 2 * CHUNK_OUT, CHUNK), jnp.float32)
    weights_hi, weights_lo = split(jnp.concatenate([main, gap, rim], axis=0).T)
    weights = jnp.concatenate([weights_hi, weights_lo], axis=1)

    def filtered(stacked):
        high, low = split(stacked)
        both = dot(high, weights)
        return both[:, :LANES] + both[:, LANES:] + dot(low, weights_hi)

    for copy in copies[1:]:
        copy.wait()
    for slot in range(slots):
        pick = picks_ref[0, slot]
        alive = alive_ref[0, pick].astype(jnp.float32)
        for j in range(chunks):
            at = SUBLANES * slot + j
            span = slice(CHUNK * j, CHUNK * (j + 1))
            source_ref[at : at + 1, :] = raw_ref[pl.ds(pick, 1), span] * alive
    high, low = split(source_ref[...])
    count = slots * SUBLANES
    both = dot(jnp.concatenate([high, low], axis=0), weights)
    sources = both[:count, :LANES] + both[:count, LANES:] + both[count:, :LANES]
    lane = lax.broadcasted_iota(jnp.int32, (SUBLANES, LANES), 1)
    row = lax.broadcasted_iota(jnp.int32, (SUBLANES, LANES), 0)
    leads = row % per_tile == 0
    wraps = lane >= LANES - EDGE
    piece = []
    rims = jnp.zeros((1, LANES), jnp.float32)
    for slot in range(slots):
        source = sources[SUBLANES * slot : SUBLANES * (slot + 1)]
        placed = source
        for step in range(1, per_tile):
            rolled = pltpu.roll(source, CHUNK_OUT * step, 1)
            placed = jnp.where(row % per_tile == step, rolled, placed)
        own = jnp.where(leads & wraps, 0.0, placed)
        rim = placed - own
        for tile in range(tiles):
            first = per_tile * tile
            inside = jnp.where((row >= first) & (row < first + per_tile), own, 0.0)
            before = jnp.where(row == first + per_tile, rim, 0.0)
            piece.append(jnp.sum(inside + before, axis=0, keepdims=True))
        rims = rims + pltpu.roll(rim[:1], LANES - EDGE * slot if slot else 0, 1)
    piece.append(rims)
    size = len(piece)
    spread = [jnp.broadcast_to(value, (SUBLANES, LANES)) for value in piece]
    eight = []
    for group in range(size):
        place = (row + SUBLANES * group) % size
        total = spread[0]
        for at in range(1, size):
            total = jnp.where(place == at, spread[at], total)
        eight.append(total)
    eight = jnp.concatenate(eight, axis=0)
    for at in range(0, pieces_ref.shape[0], SUBLANES * size):
        pieces_ref[at : at + SUBLANES * size, :] = eight
    sending = pltpu.make_async_copy(pieces_ref, pieces_hbm, sems.at[0])
    sending.start()

    result = filtered(
        jnp.concatenate(
            [raw_ref[:, CHUNK * j : CHUNK * (j + 1)] for j in range(chunks)], axis=0
        )
    )
    part = [result[rows * j : rows * (j + 1)] for j in range(chunks)]
    is_main = lax.broadcasted_iota(jnp.int32, (rows, LANES), 1) < LANES // 2
    values = []
    for first in range(0, chunks, per_tile):
        total = jnp.where(is_main, part[first], 0.0)
        for step in range(1, min(per_tile, chunks - first)):
            total = total + pltpu.roll(part[first + step], CHUNK_OUT * step, 1)
        if first + per_tile < chunks:
            total = total + jnp.where(is_main, 0.0, part[first + per_tile])
        values.append(total)
    rim = jnp.where(is_main, 0.0, part[0])
    if paired:
        packed = rim[:SUBLANES]
        for at in range(1, rows // SUBLANES):
            group = rim[SUBLANES * at : SUBLANES * (at + 1)]
            packed = packed + pltpu.roll(group, LANES - EDGE * at, 1)
        for at, value in enumerate(values):
            out_ref[rows * at : rows * (at + 1), :] = value
        out_ref[rows * tiles :, :] = packed
    else:
        for at, value in enumerate(values + [rim]):
            out_ref[:, LANES * at : LANES * (at + 1)] = value
    sending.wait()


def unpack(packed, rows):
    tiles = [packed[at : at + rows] for at in range(0, packed.shape[0] - SUBLANES, rows)]
    rims = packed[packed.shape[0] - SUBLANES :]
    rim = jnp.concatenate(
        [rims]
        + [pltpu.roll(rims, EDGE * at, 1) for at in range(1, rows // SUBLANES)],
        axis=0,
    )
    lane = lax.broadcasted_iota(jnp.int32, rim.shape, 1)
    return tiles + [jnp.where(lane >= LANES - EDGE, rim, 0.0)]


def transform(early, late, table_hi, table_lo):
    rows = early.shape[0]
    high, low = split(jnp.concatenate([early, late], axis=0))
    first = dot(jnp.concatenate([high, low], axis=0), table_hi)
    both = first[: 2 * rows] + first[2 * rows :] + dot(high, table_lo)
    quarter = lax.broadcasted_iota(jnp.int32, (1, BINS), 1) & 3
    cosine = jnp.where(quarter == 0, 1.0, 0.0) - jnp.where(quarter == 2, 1.0, 0.0)
    sine = jnp.where(quarter == 1, 1.0, 0.0) - jnp.where(quarter == 3, 1.0, 0.0)
    early_re, early_im = both[:rows, :BINS], both[:rows, BINS:]
    late_re, late_im = both[rows:, :BINS], both[rows:, BINS:]
    return (
        early_re + cosine * late_re + sine * late_im,
        early_im + cosine * late_im - sine * late_re,
    )


def whitening(real_part, imag_part, band):
    rows = real_part.shape[0]
    tiles = BINS // LANES
    stacked = []
    for part in split(real_part * real_part + imag_part * imag_part):
        zero = jnp.zeros((rows, LANES), part.dtype)
        wide = jnp.concatenate([zero, part, zero], axis=1)
        stacked += [wide[:, LANES * tile : LANES * (tile + 3)] for tile in range(tiles)]
    banded = dot(jnp.concatenate(stacked, axis=0), band)
    step = rows * tiles
    summed = banded[:step] + banded[step:]
    total = jnp.concatenate(
        [summed[rows * tile : rows * (tile + 1)] for tile in range(tiles)], axis=1
    )
    bins = lax.broadcasted_iota(jnp.int32, (1, BINS), 1)
    count = jnp.minimum(bins + HALF, BINS - 1) - jnp.maximum(bins - HALF, 0) + 1
    return lax.rsqrt(total * (1.0 / count.astype(jnp.float32)) + 1e-06)


def prepare_kernel(
    _, alive_hbm, picks_hbm, fwd_hi_hbm, fwd_lo_hbm, band_hbm, lag_hbm,
    hi_ref, lo_ref, band_ref, lag_ref, alive_out, picks_out, alive_ref, picks_ref, sems,
):
    copies = start_copies(
        [
            (alive_hbm, alive_ref),
            (picks_hbm, picks_ref),
            (fwd_hi_hbm, hi_ref),
            (fwd_lo_hbm, lo_ref),
            (band_hbm, band_ref),
            (lag_hbm, lag_ref),
        ],
        sems,
    )
    for copy in copies[:2]:
        copy.wait()
    rows = alive_out.shape[0]
    alive_out[...] = jnp.broadcast_to(
        column(alive_ref[...].astype(jnp.float32)), (rows, LANES)
    )
    channel = lax.broadcasted_iota(jnp.int32, (rows, LANES), 0)
    for slot in range(picks_ref.shape[1]):
        pick = jnp.broadcast_to(picks_ref[:, slot : slot + 1], (rows, LANES))
        picks_out[slot] = jnp.where(channel == pick, 1.0, 0.0)
    for copy in copies[2:]:
        copy.wait()


def spectra_kernel(series_ref, hi_ref, lo_ref, band_ref, alive_ref, *refs):
    spectra_ref = refs[-1]
    rows = alive_ref.shape[0]
    half = S // 2
    if len(refs) > 1:
        mine, other = [unpack(ref[...], rows) for ref in (series_ref, refs[0])]
        first = lax.axis_index("src") == 0
        early = [jnp.where(first, a, b) for a, b in zip(mine, other)]
        late = [jnp.where(first, b, a) for a, b in zip(mine, other)]
        early[-2] = early[-2] + late[-1]
        early, late = [jnp.concatenate(tiles[:-1], axis=1) for tiles in (early, late)]
    else:
        early, late = series_ref[:, :half], series_ref[:, half:]
    real_part, imag_part = transform(early, late, hi_ref[...], lo_ref[...])
    factor = alive_ref[:, :1] * whitening(real_part, imag_part, band_ref[...])
    spectra_ref[:, :BINS] = real_part * factor
    spectra_ref[:, BINS:] = imag_part * factor


def part_bounds(total):
    ends = [3 * total // 8, 3 * total // 4, total]
    return [(a, b) for a, b in zip([0] + ends, ends) if b > a]


def correlate_kernel(
    slots, spectra_ref, pieces_ref, picks_ref, hi_ref, lo_ref, band_ref, lag_ref, out_hbm,
    series_ref, rims_ref, source_ref, cross_ref, out_ref, sems,
):
    rows = spectra_ref.shape[0]
    group = out_ref.shape[0] // slots
    half = BINS // LANES
    own = lax.axis_index("blk")
    base = lax.axis_index("src") * group
    tiles = S // 2 // LANES

    for slot in range(slots):
        for block in range(group):
            row = slice(slot * group + block, slot * group + block + 1)
            at = pieces_ref.shape[0] - 1 - 2 * (base + block)
            for tile in range(tiles):
                span = slice(LANES * (slot * tiles + tile), LANES * (slot * tiles + tile + 1))
                early = slice(LANES * tile, LANES * (tile + 1))
                late = slice(S // 2 + LANES * tile, S // 2 + LANES * (tile + 1))
                series_ref[row, early] = pieces_ref[at, :, span]
                series_ref[row, late] = pieces_ref[at - 1, :, span]
            rims_ref[row, :] = pieces_ref[at - 1, :, LANES * slots * tiles :]
    rims = jnp.concatenate(
        [
            pltpu.roll(rims_ref[slot * group : (slot + 1) * group, :], EDGE * slot, 1)
            for slot in range(slots)
        ],
        axis=0,
    )
    lane = lax.broadcasted_iota(jnp.int32, rims.shape, 1)
    seam = slice(S // 2 - LANES, S // 2)
    series_ref[:, seam] = series_ref[:, seam] + jnp.where(lane >= LANES - EDGE, rims, 0.0)
    early, late = series_ref[:, : S // 2], series_ref[:, S // 2 :]
    real_part, imag_part = transform(early, late, hi_ref[...], lo_ref[...])
    factor = whitening(real_part, imag_part, band_ref[...])
    source_ref[:, :BINS] = real_part * factor
    source_ref[:, BINS:] = imag_part * factor
    copies = []
    for part, (first, last) in enumerate(part_bounds(group * slots)):
        per_part = last - first
        for tile in range(half):
            re = slice(LANES * tile, LANES * (tile + 1))
            im = slice(BINS + LANES * tile, BINS + LANES * (tile + 1))
            rec_re, rec_im = spectra_ref[:, re], spectra_ref[:, im]
            for source in range(first, first + per_part):
                block, slot = divmod(source, slots)
                at = slot * group + block
                src_re, src_im = source_ref[at : at + 1, re], source_ref[at : at + 1, im]
                where = slice(rows * source, rows * (source + 1))
                cross_ref[where, re] = (src_re * rec_re + src_im * rec_im).astype(jnp.bfloat16)
                cross_ref[where, im] = (src_re * rec_im - src_im * rec_re).astype(jnp.bfloat16)
        lagged = dot(cross_ref[rows * first : rows * (first + per_part), :], lag_ref[...])
        for source in range(first, first + per_part):
            block, slot = divmod(source, slots)
            keep = 1.0 - jnp.where(own == base + block, 1.0, 0.0) * picks_ref[slot]
            at = source - first
            kept = lagged[rows * at : rows * (at + 1)] * jnp.concatenate(
                [keep] * (LAGS // LANES), axis=1
            )
            out_ref[source] = kept.astype(jnp.bfloat16)
        span = pl.ds(first, per_part)
        copies.append(pltpu.make_async_copy(out_ref.at[span], out_hbm.at[span], sems.at[part]))
        copies[-1].start()
    for copy in copies:
        copy.wait()


HBM = pl.BlockSpec(memory_space=pltpu.HBM)
VMEM = pl.BlockSpec(memory_space=pltpu.VMEM)
PARAMS = pltpu.CompilerParams(vmem_limit_bytes=VMEM_LIMIT)


def in_hbm(*arrays):
    return [pltpu.with_memory_space_constraint(array, pltpu.HBM) for array in arrays]


def shaped(*shape, dtype=jnp.float32):
    return jax.ShapeDtypeStruct(shape, dtype)


def local(raw_records, fir_taps, alive_mask, source_index):
    src_count = lax.axis_size("src")
    blk_count = lax.axis_size("blk")
    rows, raw_count = raw_records.shape
    slots = source_index.shape[1]
    group = blk_count // src_count
    out_count = raw_count // DEC
    width = -(-out_count // LANES) * LANES + LANES
    chunks = raw_count // CHUNK
    paired = src_count == 2 and 2 * out_count == S
    bf16 = jnp.bfloat16
    forward_hi, forward_lo = split_table(forward_table())
    alive_row = alive_mask.reshape(1, rows)

    with jax.named_scope("decimate"):
        device_count = blk_count * src_count
        main = slots * (width - LANES)
        decimated, pieces = pl.pallas_call(
            lambda *refs: decimate_kernel(paired, *refs),
            out_shape=(
                shaped(rows * (S // 2 // LANES) + SUBLANES, LANES)
                if paired
                else shaped(rows, width),
                shaped(device_count * (main // LANES + 1), LANES),
            ),
            in_specs=[HBM] * 4,
            out_specs=(VMEM, HBM),
            scratch_shapes=[
                pltpu.VMEM((rows, raw_count), jnp.float32),
                pltpu.VMEM((1, TAPS), jnp.float32),
                pltpu.SMEM((1, rows), jnp.int32),
                pltpu.SMEM((1, slots), jnp.int32),
                pltpu.VMEM((SUBLANES * slots, CHUNK), jnp.float32),
                pltpu.VMEM((device_count * (main // LANES + 1), LANES), jnp.float32),
                pltpu.SemaphoreType.DMA((rows // SUBLANES + 3,)),
            ],
            compiler_params=PARAMS,
        )(*in_hbm(raw_records, fir_taps.reshape(1, TAPS), alive_row, source_index))

    def whole(shards):
        rims = jnp.pad(shards[1:, :, width - EDGE :], ((0, 1), (0, 0), (out_count - EDGE, 0)))
        series = shards[:, :, :out_count] + rims
        return series.transpose(1, 0, 2).reshape(shards.shape[1], S)

    with jax.named_scope("gather_sources"):
        gathered = lax.all_to_all(
            pieces.reshape(device_count, 1, main + LANES),
            ("blk", "src"),
            split_axis=0,
            concat_axis=0,
            tiled=True,
            axis_index_groups=[list(reversed(range(device_count)))],
        )
        if not paired:
            gathered = gathered[::-1]
            shards = gathered.reshape(blk_count, src_count, main + LANES)
            shards = shards.transpose(1, 0, 2)
            rims = [shards[:, :, main + LANES - EDGE * (slot + 1) :] for slot in range(slots)]
            rims = jnp.stack([rim[:, :, :EDGE] for rim in rims], axis=2)
            rims = jnp.pad(rims, ((0, 0), (0, 0), (0, 0), (LANES - EDGE, 0)))
            series = shards[:, :, :main].reshape(src_count, blk_count, slots, width - LANES)
            series = jnp.concatenate([series, rims], axis=3)
            series = whole(series.reshape(src_count, blk_count * slots, width))
            series = series.reshape(blk_count, slots, 2, S // 2).transpose(0, 2, 1, 3)
            series = series.reshape(blk_count * 2, 1, slots * S // 2)
            gathered = jnp.pad(series, ((0, 0), (0, 0), (0, LANES)))[::-1]

    with jax.named_scope("prepare"):
        out_shape = (
            shaped(S // 2, NFFT, dtype=bf16),
            shaped(S // 2, NFFT, dtype=bf16),
            shaped(3 * LANES, LANES, dtype=bf16),
            shaped(NFFT, LAGS, dtype=bf16),
            shaped(rows, LANES),
            shaped(slots, rows, LANES),
        )
        table_hi, table_lo, band, lag, alive, picks = pl.pallas_call(
            prepare_kernel,
            out_shape=out_shape,
            in_specs=[VMEM] + [HBM] * 6,
            out_specs=(VMEM,) * len(out_shape),
            scratch_shapes=[
                pltpu.VMEM((1, rows), jnp.int32),
                pltpu.VMEM((1, slots), jnp.int32),
                pltpu.SemaphoreType.DMA((6,)),
            ],
            compiler_params=PARAMS,
            cost_estimate=pl.CostEstimate(
                flops=0, bytes_accessed=4 * S * NFFT, transcendentals=0
            ),
        )(
            decimated,
            *in_hbm(
                alive_row,
                source_index,
                jnp.asarray(forward_hi),
                jnp.asarray(forward_lo),
                jnp.asarray(band_table()),
                jnp.asarray(lag_table()),
            ),
        )

    with jax.named_scope("regroup"):
        if paired:
            series = [decimated]
            other = [lax.ppermute(decimated, "src", [(0, 1), (1, 0)])]
        else:
            series = [whole(lax.all_gather(decimated, "src", axis=0))]
            other = []

    with jax.named_scope("spectra"):
        operands = series + [table_hi, table_lo, band, alive] + other
        spectra = pl.pallas_call(
            spectra_kernel,
            out_shape=shaped(rows, NFFT),
            in_specs=[VMEM] * len(operands),
            out_specs=VMEM,
            compiler_params=PARAMS,
        )(*operands)

    with jax.named_scope("correlate"):
        total = group * slots
        return pl.pallas_call(
            lambda *refs: correlate_kernel(slots, *refs),
            out_shape=shaped(total, rows, LAGS, dtype=bf16),
            in_specs=[VMEM] * 7,
            out_specs=HBM,
            scratch_shapes=[
                pltpu.VMEM((total, S), jnp.float32),
                pltpu.VMEM((total, LANES), jnp.float32),
                pltpu.VMEM((total, NFFT), jnp.float32),
                pltpu.VMEM((total * rows, NFFT), bf16),
                pltpu.VMEM((total, rows, LAGS), bf16),
                pltpu.SemaphoreType.DMA((PARTS,)),
            ],
            compiler_params=PARAMS,
        )(spectra, gathered, picks, table_hi, table_lo, band, lag)


def solution(mesh):
    in_specs = (P("blk", "src"), P(), P("blk"), P("blk", None))
    out_specs = P("src", "blk", None)
    return jax.shard_map(local, mesh=mesh, in_specs=in_specs, out_specs=out_specs, check_vma=False)
```

profile of v0, /device:TPU:0, one launch (start us, length us, event | category | flops | bytes accessed | tf_op | source)
XLA Modules:
  0.0 18.7 jit_solution(4776942198041732993)
XLA Ops:
  0.0 2.3 %decimate.1 = (f32[72,128]{1,0:T(8,128)S(1)}, f32[160,128]{1,0:T(8,128)}) custom-call(f32[32,5120]{1,0:T(8,128)} %refs_0_.1, f32[1,64]{1,0:T(1,128)} %bitcast.5, s32[1,32]{1,0:T(1,128)} %bitcast.3, s32[1,2]{1,0:T(1,128)} %picks_hbm.1), custom_call_target="tpu_custom_call" | custom-call | tf_op jit(solution)/shard_map/decimate/pallas_call | solution.py:392
  2.3 7.3 %all-to-all-start = ((f32[32,1,640]{2,1,0:T(1,128)}), f32[32,1,640]{2,1,0:T(1,128)S(1)}, u32[]{:S(2)}, u32[]{:S(2)}) async-start(f32[32,1,640]{2,1,0:T(1,128)} %bitcast.2), calls=%async_computation | async-start | bytes 163840 | tf_op jit(solution)/shard_map/gather_sources/all_to_all | solution.py:420
  9.6 1.8 %collective-permute-start = (f32[72,128]{1,0:T(8,128)S(1)}, f32[72,128]{1,0:T(8,128)S(1)}, u32[]{:S(2)}, u32[]{:S(2)}) collective-permute-start(f32[72,128]{1,0:T(8,128)S(1)} %get-tuple-element.13._.series_ref), channel_id=1, source_target_pairs={{0,1},{1,0},{2,3},{3,2},{4,5},{5,4},{6,7},{7,6},{8,9},{9,8},{10,11... | collective-permute-start | bytes 110600 | tf_op jit(solution)/shard_map/regroup/ppermute | solution.py:480
  11.4 1.7 %prepare.1 = (bf16[256,1024]{1,0:T(8,128)(2,1)S(1)}, bf16[256,1024]{1,0:T(8,128)(2,1)S(1)}, bf16[384,128]{1,0:T(8,128)(2,1)S(1)}, bf16[1024,512]{1,0:T(8,128)(2,...) custom-call(f32[72,128]{1,0:T(8,128)S(1)} %get-tuple-element.13._.series_ref, s32[1,32]{1,0:T(1,128)} %bitcast.4, ...), custom_call_target="tpu_custom_call" | custom-call | bytes 2097152 | tf_op jit(solution)/shard_map/prepare/pallas_call | solution.py:451
  13.1 0.6 %collective-permute-done.refs_0_ = f32[72,128]{1,0:T(8,128)S(1)} collective-permute-done((f32[72,128]{1,0:T(8,128)S(1)}, f32[72,128]{1,0:T(8,128)S(1)}, u32[]{:S(2)}, u32[]{:S(2)}) %collective-permute-start) | collective-permute-done | bytes 36896 | tf_op jit(solution)/shard_map/regroup/ppermute | solution.py:480
  13.7 0.5 %spectra.1.refs_0_ = f32[32,1024]{1,0:T(8,128)S(1)} custom-call(f32[72,128]{1,0:T(8,128)S(1)} %get-tuple-element.13._.series_ref, bf16[256,1024]{1,0:T(8,128)(2,1)S(1)} %get-tuple-element.14.hi_ref.refs_3_, bf16[256,1024]{1,0:T(8,128)(2,1)S(1)} %get-tuple-element.15.lo_ref.refs_4_, bf16[384,128]{1,0:T(8,128)(2,1)S(1)} %get-tuple-element.16.band_ref.refs_5_, ...), custom_call_target="tpu_custom_call" | custom-call | tf_op jit(solution)/shard_map/spectra/pallas_call | solution.py:487
  14.3 2.4 %all-to-all-done.refs_1_ = f32[32,1,640]{2,1,0:T(1,128)S(1)} async-done(((f32[32,1,640]{2,1,0:T(1,128)}), f32[32,1,640]{2,1,0:T(1,128)S(1)}, u32[]{:S(2)}, u32[]{:S(2)}) %all-to-all-start) | async-done | bytes 81952 | tf_op jit(solution)/shard_map/gather_sources/all_to_all | solution.py:420
  16.7 2.0 %correlate.1 = bf16[16,32,512]{2,1,0:T(8,128)(2,1)} custom-call(f32[32,1024]{1,0:T(8,128)S(1)} %spectra.1.refs_0_, f32[32,1,640]{2,1,0:T(1,128)S(1)} %all-to-all-done.refs_1_, f32[2,32,128]{2,1,0:T(8,128)S(1)} %get-tuple-element.19.refs_2_, bf16[256,1024]{1,0:T(8,128)(2,1)S(1)} %get-tuple-element.14.hi_ref.refs_3_, ...), custom_call_target="tpu_custom_call" | custom-call | tf_op jit(solution)/shard_map/correlate/pallas_call | solution.py:497
Async XLA Ops:
  2.3 14.4 %all-to-all-start = ((f32[32,1,640]{2,1,0:T(1,128)}), f32[32,1,640]{2,1,0:T(1,128)S(1)}, u32[]{:S(2)}, u32[]{:S(2)}) async-start(f32[32,1,640]{2,1,0:T(1,128)} %bitcast.2), calls=%async_computation | async-start | bytes 163840 | tf_op jit(solution)/shard_map/gather_sources/all_to_all | solution.py:420
  9.6 4.1 %collective-permute-start = (f32[72,128]{1,0:T(8,128)S(1)}, f32[72,128]{1,0:T(8,128)S(1)}, u32[]{:S(2)}, u32[]{:S(2)}) collective-permute-start(f32[72,128]{1,0:T(8,128)S(1)} %get-tuple-element.13._.series_ref), channel_id=1, source_target_pairs={{0,1},{1,0},{2,3},{3,2},{4,5},{5,4},{6,7},{7,6},{8,9},{9,8},{10,11... | collective-permute-start | bytes 110600 | tf_op jit(solution)/shard_map/regroup/ppermute | solution.py:480
where the time goes:
time: 18.9 us; the launch traced here: 18.7 us
  starting transfers between devices  9.14 us (48%)
  Pallas kernels  6.41 us (34%)
  waiting for transfers between devices  3.09 us (16%)
    all_to_all x1, starting transfers between devices, local(): lax.all_to_all(pieces.reshape(device_count, 1, main + LANES), ('blk', 'sr...  7.3 us
    all_to_all x1, waiting for transfers between devices, local(): lax.all_to_all(pieces.reshape(device_count, 1, main + LANES), ('blk', 'sr...  2.45 us
    pallas_call x1, Pallas kernels, local(): pl.pallas_call(lambda *refs: decimate_kernel(paired, *refs), out_shape=(s...  2.25 us
    pallas_call x1, Pallas kernels, local(): pl.pallas_call(lambda *refs: correlate_kernel(slots, *refs), out_shape=sh...  1.96 us
    ppermute x1, starting transfers between devices, local(): other = [lax.ppermute(decimated, 'src', [(0, 1), (1, 0)])]  1.83 us
    pallas_call x1, Pallas kernels, local(): pl.pallas_call(prepare_kernel, out_shape=out_shape, in_specs=[VMEM] + [HB...  1.65 us
    ppermute x1, waiting for transfers between devices, local(): other = [lax.ppermute(decimated, 'src', [(0, 1), (1, 0)])]  0.64 us
    pallas_call x1, Pallas kernels, local(): pl.pallas_call(spectra_kernel, out_shape=shaped(rows, NFFT), in_specs=[VM...  0.54 us
  transfers between devices with their start and end apart: 2, of which 2 were waited for; matrix products, arithmetic and copies ran while one was open for 0% of the time, Pallas kernels for 12%

commit v1 on v0

--- a/solution.py
+++ b/solution.py
@@ -17,7 +17,7 @@
 HALF = 64
 LANES = 128
 SUBLANES = 8
-PARTS = 3
+PARTS = 4
 EDGE = (TAPS - 1) // DEC
 CHUNK = 640
 CHUNK_OUT = CHUNK // DEC
@@ -287,11 +287,6 @@
     spectra_ref[:, BINS:] = imag_part * factor
 
 
-def part_bounds(total):
-    ends = [3 * total // 8, 3 * total // 4, total]
-    return [(a, b) for a, b in zip([0] + ends, ends) if b > a]
-
-
 def correlate_kernel(
     slots, spectra_ref, pieces_ref, picks_ref, hi_ref, lo_ref, band_ref, lag_ref, out_hbm,
     series_ref, rims_ref, source_ref, cross_ref, out_ref, sems,
@@ -329,26 +324,27 @@
     factor = whitening(real_part, imag_part, band_ref[...])
     source_ref[:, :BINS] = real_part * factor
     source_ref[:, BINS:] = imag_part * factor
+    total = group * slots
+    for tile in range(half):
+        re = slice(LANES * tile, LANES * (tile + 1))
+        im = slice(BINS + LANES * tile, BINS + LANES * (tile + 1))
+        rec_re, rec_im = spectra_ref[:, re], spectra_ref[:, im]
+        for source in range(total):
+            block, slot = divmod(source, slots)
+            at = slot * group + block
+            src_re, src_im = source_ref[at : at + 1, re], source_ref[at : at + 1, im]
+            where = slice(rows * source, rows * (source + 1))
+            cross_ref[where, re] = (src_re * rec_re + src_im * rec_im).astype(jnp.bfloat16)
+            cross_ref[where, im] = (src_re * rec_im - src_im * rec_re).astype(jnp.bfloat16)
+    lagged = dot(cross_ref[...], lag_ref[...])
     copies = []
-    for part, (first, last) in enumerate(part_bounds(group * slots)):
-        per_part = last - first
-        for tile in range(half):
-            re = slice(LANES * tile, LANES * (tile + 1))
-            im = slice(BINS + LANES * tile, BINS + LANES * (tile + 1))
-            rec_re, rec_im = spectra_ref[:, re], spectra_ref[:, im]
-            for source in range(first, first + per_part):
-                block, slot = divmod(source, slots)
-                at = slot * group + block
-                src_re, src_im = source_ref[at : at + 1, re], source_ref[at : at + 1, im]
-                where = slice(rows * source, rows * (source + 1))
-                cross_ref[where, re] = (src_re * rec_re + src_im * rec_im).astype(jnp.bfloat16)
-                cross_ref[where, im] = (src_re * rec_im - src_im * rec_re).astype(jnp.bfloat16)
-        lagged = dot(cross_ref[rows * first : rows * (first + per_part), :], lag_ref[...])
+    per_part = max(1, total // PARTS)
+    for part in range(total // per_part):
+        first = part * per_part
         for source in range(first, first + per_part):
             block, slot = divmod(source, slots)
             keep = 1.0 - jnp.where(own == base + block, 1.0, 0.0) * picks_ref[slot]
-            at = source - first
-            kept = lagged[rows * at : rows * (at + 1)] * jnp.concatenate(
+            kept = lagged[rows * source : rows * (source + 1)] * jnp.concatenate(
                 [keep] * (LAGS // LANES), axis=1
             )
             out_ref[source] = kept.astype(jnp.bfloat16)

time: 18.9 us -> 18.9 us (level)
  no operation moved by 1% of the time
where the time goes in v1:
time: 18.9 us; the launch traced here: 18.7 us
  starting transfers between devices  9.14 us (48%)
  Pallas kernels  6.4 us (34%)
  waiting for transfers between devices  3.09 us (16%)
    all_to_all x1, starting transfers between devices, local(): lax.all_to_all(pieces.reshape(device_count, 1, main + LANES), ('blk', 'sr...  7.3 us
    all_to_all x1, waiting for transfers between devices, local(): lax.all_to_all(pieces.reshape(device_count, 1, main + LANES), ('blk', 'sr...  2.45 us
    pallas_call x1, Pallas kernels, local(): pl.pallas_call(lambda *refs: decimate_kernel(paired, *refs), out_shape=(s...  2.25 us
    pallas_call x1, Pallas kernels, local(): pl.pallas_call(lambda *refs: correlate_kernel(slots, *refs), out_shape=sh...  1.96 us
    ppermute x1, starting transfers between devices, local(): other = [lax.ppermute(decimated, 'src', [(0, 1), (1, 0)])]  1.83 us
    pallas_call x1, Pallas kernels, local(): pl.pallas_call(prepare_kernel, out_shape=out_shape, in_specs=[VMEM] + [HB...  1.65 us
    ppermute x1, waiting for transfers between devices, local(): other = [lax.ppermute(decimated, 'src', [(0, 1), (1, 0)])]  0.64 us
    pallas_call x1, Pallas kernels, local(): pl.pallas_call(spectra_kernel, out_shape=shaped(rows, NFFT), in_specs=[VM...  0.54 us
  transfers between devices with their start and end apart: 2, of which 2 were waited for; matrix products, arithmetic and copies ran while one was open for 0% of the time, Pallas kernels for 12%

profile of v1, /device:TPU:0, one launch (start us, length us, event | category | flops | bytes accessed | tf_op | source)
XLA Modules:
  0.0 18.7 jit_solution(3233772053853790186)
XLA Ops:
  0.0 2.3 %decimate.1 = (f32[72,128]{1,0:T(8,128)S(1)}, f32[160,128]{1,0:T(8,128)}) custom-call(f32[32,5120]{1,0:T(8,128)} %refs_0_.1, f32[1,64]{1,0:T(1,128)} %bitcast.5, s32[1,32]{1,0:T(1,128)} %bitcast.3, s32[1,2]{1,0:T(1,128)} %picks_hbm.1), custom_call_target="tpu_custom_call" | custom-call | tf_op jit(solution)/shard_map/decimate/pallas_call | solution.py:388
  2.3 7.3 %all-to-all-start = ((f32[32,1,640]{2,1,0:T(1,128)}), f32[32,1,640]{2,1,0:T(1,128)S(1)}, u32[]{:S(2)}, u32[]{:S(2)}) async-start(f32[32,1,640]{2,1,0:T(1,128)} %bitcast.2), calls=%async_computation | async-start | bytes 163840 | tf_op jit(solution)/shard_map/gather_sources/all_to_all | solution.py:416
  9.6 1.8 %collective-permute-start = (f32[72,128]{1,0:T(8,128)S(1)}, f32[72,128]{1,0:T(8,128)S(1)}, u32[]{:S(2)}, u32[]{:S(2)}) collective-permute-start(f32[72,128]{1,0:T(8,128)S(1)} %get-tuple-element.13._.series_ref), channel_id=1, source_target_pairs={{0,1},{1,0},{2,3},{3,2},{4,5},{5,4},{6,7},{7,6},{8,9},{9,8},{10,11... | collective-permute-start | bytes 110600 | tf_op jit(solution)/shard_map/regroup/ppermute | solution.py:476
  11.4 1.7 %prepare.1 = (bf16[256,1024]{1,0:T(8,128)(2,1)S(1)}, bf16[256,1024]{1,0:T(8,128)(2,1)S(1)}, bf16[384,128]{1,0:T(8,128)(2,1)S(1)}, bf16[1024,512]{1,0:T(8,128)(2,...) custom-call(f32[72,128]{1,0:T(8,128)S(1)} %get-tuple-element.13._.series_ref, s32[1,32]{1,0:T(1,128)} %bitcast.4, ...), custom_call_target="tpu_custom_call" | custom-call | bytes 2097152 | tf_op jit(solution)/shard_map/prepare/pallas_call | solution.py:447
  13.1 0.6 %collective-permute-done.refs_0_ = f32[72,128]{1,0:T(8,128)S(1)} collective-permute-done((f32[72,128]{1,0:T(8,128)S(1)}, f32[72,128]{1,0:T(8,128)S(1)}, u32[]{:S(2)}, u32[]{:S(2)}) %collective-permute-start) | collective-permute-done | bytes 36896 | tf_op jit(solution)/shard_map/regroup/ppermute | solution.py:476
  13.7 0.5 %spectra.1.refs_0_ = f32[32,1024]{1,0:T(8,128)S(1)} custom-call(f32[72,128]{1,0:T(8,128)S(1)} %get-tuple-element.13._.series_ref, bf16[256,1024]{1,0:T(8,128)(2,1)S(1)} %get-tuple-element.14.hi_ref.refs_3_, bf16[256,1024]{1,0:T(8,128)(2,1)S(1)} %get-tuple-element.15.lo_ref.refs_4_, bf16[384,128]{1,0:T(8,128)(2,1)S(1)} %get-tuple-element.16.band_ref.refs_5_, ...), custom_call_target="tpu_custom_call" | custom-call | tf_op jit(solution)/shard_map/spectra/pallas_call | solution.py:483
  14.3 2.4 %all-to-all-done.refs_1_ = f32[32,1,640]{2,1,0:T(1,128)S(1)} async-done(((f32[32,1,640]{2,1,0:T(1,128)}), f32[32,1,640]{2,1,0:T(1,128)S(1)}, u32[]{:S(2)}, u32[]{:S(2)}) %all-to-all-start) | async-done | bytes 81952 | tf_op jit(solution)/shard_map/gather_sources/all_to_all | solution.py:416
  16.7 2.0 %correlate.1 = bf16[16,32,512]{2,1,0:T(8,128)(2,1)} custom-call(f32[32,1024]{1,0:T(8,128)S(1)} %spectra.1.refs_0_, f32[32,1,640]{2,1,0:T(1,128)S(1)} %all-to-all-done.refs_1_, f32[2,32,128]{2,1,0:T(8,128)S(1)} %get-tuple-element.19.refs_2_, bf16[256,1024]{1,0:T(8,128)(2,1)S(1)} %get-tuple-element.14.hi_ref.refs_3_, ...), custom_call_target="tpu_custom_call" | custom-call | tf_op jit(solution)/shard_map/correlate/pallas_call | solution.py:493
Async XLA Ops:
  2.3 14.4 %all-to-all-start = ((f32[32,1,640]{2,1,0:T(1,128)}), f32[32,1,640]{2,1,0:T(1,128)S(1)}, u32[]{:S(2)}, u32[]{:S(2)}) async-start(f32[32,1,640]{2,1,0:T(1,128)} %bitcast.2), calls=%async_computation | async-start | bytes 163840 | tf_op jit(solution)/shard_map/gather_sources/all_to_all | solution.py:416
  9.6 4.1 %collective-permute-start = (f32[72,128]{1,0:T(8,128)S(1)}, f32[72,128]{1,0:T(8,128)S(1)}, u32[]{:S(2)}, u32[]{:S(2)}) collective-permute-start(f32[72,128]{1,0:T(8,128)S(1)} %get-tuple-element.13._.series_ref), channel_id=1, source_target_pairs={{0,1},{1,0},{2,3},{3,2},{4,5},{5,4},{6,7},{7,6},{8,9},{9,8},{10,11... | collective-permute-start | bytes 110600 | tf_op jit(solution)/shard_map/regroup/ppermute | solution.py:476

commit v2 on v0

--- a/solution.py
+++ b/solution.py
@@ -17,7 +17,7 @@
 HALF = 64
 LANES = 128
 SUBLANES = 8
-PARTS = 3
+PARTS = 4
 EDGE = (TAPS - 1) // DEC
 CHUNK = 640
 CHUNK_OUT = CHUNK // DEC
@@ -287,14 +287,9 @@
     spectra_ref[:, BINS:] = imag_part * factor
 
 
-def part_bounds(total):
-    ends = [3 * total // 8, 3 * total // 4, total]
-    return [(a, b) for a, b in zip([0] + ends, ends) if b > a]
-
-
 def correlate_kernel(
     slots, spectra_ref, pieces_ref, picks_ref, hi_ref, lo_ref, band_ref, lag_ref, out_hbm,
-    series_ref, rims_ref, source_ref, cross_ref, out_ref, sems,
+    series_ref, rims_ref, source_ref, out_ref, sems, *cross_refs,
 ):
     rows = spectra_ref.shape[0]
     group = out_ref.shape[0] // slots
@@ -329,21 +324,28 @@
     factor = whitening(real_part, imag_part, band_ref[...])
     source_ref[:, :BINS] = real_part * factor
     source_ref[:, BINS:] = imag_part * factor
-    copies = []
-    for part, (first, last) in enumerate(part_bounds(group * slots)):
-        per_part = last - first
+    def make_cross(part):
+        cross_ref = cross_refs[part]
         for tile in range(half):
             re = slice(LANES * tile, LANES * (tile + 1))
             im = slice(BINS + LANES * tile, BINS + LANES * (tile + 1))
             rec_re, rec_im = spectra_ref[:, re], spectra_ref[:, im]
-            for source in range(first, first + per_part):
-                block, slot = divmod(source, slots)
-                at = slot * group + block
-                src_re, src_im = source_ref[at : at + 1, re], source_ref[at : at + 1, im]
-                where = slice(rows * source, rows * (source + 1))
+            for at in range(per_part):
+                block, slot = divmod(part * per_part + at, slots)
+                row = slot * group + block
+                src_re, src_im = source_ref[row : row + 1, re], source_ref[row : row + 1, im]
+                where = slice(rows * at, rows * (at + 1))
                 cross_ref[where, re] = (src_re * rec_re + src_im * rec_im).astype(jnp.bfloat16)
                 cross_ref[where, im] = (src_re * rec_im - src_im * rec_re).astype(jnp.bfloat16)
-        lagged = dot(cross_ref[rows * first : rows * (first + per_part), :], lag_ref[...])
+
+    per_part = group * slots // PARTS
+    copies = []
+    make_cross(0)
+    for part in range(PARTS):
+        if part + 1 < PARTS:
+            make_cross(part + 1)
+        lagged = dot(cross_refs[part][...], lag_ref[...])
+        first = part * per_part
         for source in range(first, first + per_part):
             block, slot = divmod(source, slots)
             keep = 1.0 - jnp.where(own == base + block, 1.0, 0.0) * picks_ref[slot]
@@ -503,10 +505,10 @@
                 pltpu.VMEM((total, S), jnp.float32),
                 pltpu.VMEM((total, LANES), jnp.float32),
                 pltpu.VMEM((total, NFFT), jnp.float32),
-                pltpu.VMEM((total * rows, NFFT), bf16),
                 pltpu.VMEM((total, rows, LAGS), bf16),
                 pltpu.SemaphoreType.DMA((PARTS,)),
-            ],
+            ]
+            + [pltpu.VMEM((total // PARTS * rows, NFFT), bf16)] * PARTS,
             compiler_params=PARAMS,
         )(spectra, gathered, picks, table_hi, table_lo, band, lag)
 

time: 18.9 us -> 18.9 us (level)
  no operation moved by 1% of the time
where the time goes in v2:
time: 18.9 us; the launch traced here: 18.7 us
  starting transfers between devices  9.14 us (48%)
  Pallas kernels  6.41 us (34%)
  waiting for transfers between devices  3.09 us (16%)
    all_to_all x1, starting transfers between devices, local(): lax.all_to_all(pieces.reshape(device_count, 1, main + LANES), ('blk', 'sr...  7.3 us
    all_to_all x1, waiting for transfers between devices, local(): lax.all_to_all(pieces.reshape(device_count, 1, main + LANES), ('blk', 'sr...  2.45 us
    pallas_call x1, Pallas kernels, local(): pl.pallas_call(lambda *refs: decimate_kernel(paired, *refs), out_shape=(s...  2.25 us
    pallas_call x1, Pallas kernels, local(): pl.pallas_call(lambda *refs: correlate_kernel(slots, *refs), out_shape=sh...  1.96 us
    ppermute x1, starting transfers between devices, local(): other = [lax.ppermute(decimated, 'src', [(0, 1), (1, 0)])]  1.83 us
    pallas_call x1, Pallas kernels, local(): pl.pallas_call(prepare_kernel, out_shape=out_shape, in_specs=[VMEM] + [HB...  1.65 us
    ppermute x1, waiting for transfers between devices, local(): other = [lax.ppermute(decimated, 'src', [(0, 1), (1, 0)])]  0.64 us
    pallas_call x1, Pallas kernels, local(): pl.pallas_call(spectra_kernel, out_shape=shaped(rows, NFFT), in_specs=[VM...  0.54 us
  transfers between devices with their start and end apart: 2, of which 2 were waited for; matrix products, arithmetic and copies ran while one was open for 0% of the time, Pallas kernels for 12%

profile of v2, /device:TPU:0, one launch (start us, length us, event | category | flops | bytes accessed | tf_op | source)
XLA Modules:
  0.0 18.7 jit_solution(16942775591830950994)
XLA Ops:
  0.0 2.3 %decimate.1 = (f32[72,128]{1,0:T(8,128)S(1)}, f32[160,128]{1,0:T(8,128)}) custom-call(f32[32,5120]{1,0:T(8,128)} %refs_0_.1, f32[1,64]{1,0:T(1,128)} %bitcast.5, s32[1,32]{1,0:T(1,128)} %bitcast.3, s32[1,2]{1,0:T(1,128)} %picks_hbm.1), custom_call_target="tpu_custom_call" | custom-call | tf_op jit(solution)/shard_map/decimate/pallas_call | solution.py:394
  2.3 7.3 %all-to-all-start = ((f32[32,1,640]{2,1,0:T(1,128)}), f32[32,1,640]{2,1,0:T(1,128)S(1)}, u32[]{:S(2)}, u32[]{:S(2)}) async-start(f32[32,1,640]{2,1,0:T(1,128)} %bitcast.2), calls=%async_computation | async-start | bytes 163840 | tf_op jit(solution)/shard_map/gather_sources/all_to_all | solution.py:422
  9.6 1.8 %collective-permute-start = (f32[72,128]{1,0:T(8,128)S(1)}, f32[72,128]{1,0:T(8,128)S(1)}, u32[]{:S(2)}, u32[]{:S(2)}) collective-permute-start(f32[72,128]{1,0:T(8,128)S(1)} %get-tuple-element.13._.series_ref), channel_id=1, source_target_pairs={{0,1},{1,0},{2,3},{3,2},{4,5},{5,4},{6,7},{7,6},{8,9},{9,8},{10,11... | collective-permute-start | bytes 110600 | tf_op jit(solution)/shard_map/regroup/ppermute | solution.py:482
  11.4 1.7 %prepare.1 = (bf16[256,1024]{1,0:T(8,128)(2,1)S(1)}, bf16[256,1024]{1,0:T(8,128)(2,1)S(1)}, bf16[384,128]{1,0:T(8,128)(2,1)S(1)}, bf16[1024,512]{1,0:T(8,128)(2,...) custom-call(f32[72,128]{1,0:T(8,128)S(1)} %get-tuple-element.13._.series_ref, s32[1,32]{1,0:T(1,128)} %bitcast.4, ...), custom_call_target="tpu_custom_call" | custom-call | bytes 2097152 | tf_op jit(solution)/shard_map/prepare/pallas_call | solution.py:453
  13.1 0.6 %collective-permute-done.refs_0_ = f32[72,128]{1,0:T(8,128)S(1)} collective-permute-done((f32[72,128]{1,0:T(8,128)S(1)}, f32[72,128]{1,0:T(8,128)S(1)}, u32[]{:S(2)}, u32[]{:S(2)}) %collective-permute-start) | collective-permute-done | bytes 36896 | tf_op jit(solution)/shard_map/regroup/ppermute | solution.py:482
  13.7 0.5 %spectra.1.refs_0_ = f32[32,1024]{1,0:T(8,128)S(1)} custom-call(f32[72,128]{1,0:T(8,128)S(1)} %get-tuple-element.13._.series_ref, bf16[256,1024]{1,0:T(8,128)(2,1)S(1)} %get-tuple-element.14.hi_ref.refs_3_, bf16[256,1024]{1,0:T(8,128)(2,1)S(1)} %get-tuple-element.15.lo_ref.refs_4_, bf16[384,128]{1,0:T(8,128)(2,1)S(1)} %get-tuple-element.16.band_ref.refs_5_, ...), custom_call_target="tpu_custom_call" | custom-call | tf_op jit(solution)/shard_map/spectra/pallas_call | solution.py:489
  14.3 2.4 %all-to-all-done.refs_1_ = f32[32,1,640]{2,1,0:T(1,128)S(1)} async-done(((f32[32,1,640]{2,1,0:T(1,128)}), f32[32,1,640]{2,1,0:T(1,128)S(1)}, u32[]{:S(2)}, u32[]{:S(2)}) %all-to-all-start) | async-done | bytes 81952 | tf_op jit(solution)/shard_map/gather_sources/all_to_all | solution.py:422
  16.7 2.0 %correlate.1 = bf16[16,32,512]{2,1,0:T(8,128)(2,1)} custom-call(f32[32,1024]{1,0:T(8,128)S(1)} %spectra.1.refs_0_, f32[32,1,640]{2,1,0:T(1,128)S(1)} %all-to-all-done.refs_1_, f32[2,32,128]{2,1,0:T(8,128)S(1)} %get-tuple-element.19.refs_2_, bf16[256,1024]{1,0:T(8,128)(2,1)S(1)} %get-tuple-element.14.hi_ref.refs_3_, ...), custom_call_target="tpu_custom_call" | custom-call | tf_op jit(solution)/shard_map/correlate/pallas_call | solution.py:499
Async XLA Ops:
  2.3 14.4 %all-to-all-start = ((f32[32,1,640]{2,1,0:T(1,128)}), f32[32,1,640]{2,1,0:T(1,128)S(1)}, u32[]{:S(2)}, u32[]{:S(2)}) async-start(f32[32,1,640]{2,1,0:T(1,128)} %bitcast.2), calls=%async_computation | async-start | bytes 163840 | tf_op jit(solution)/shard_map/gather_sources/all_to_all | solution.py:422
  9.6 4.1 %collective-permute-start = (f32[72,128]{1,0:T(8,128)S(1)}, f32[72,128]{1,0:T(8,128)S(1)}, u32[]{:S(2)}, u32[]{:S(2)}) collective-permute-start(f32[72,128]{1,0:T(8,128)S(1)} %get-tuple-element.13._.series_ref), channel_id=1, source_target_pairs={{0,1},{1,0},{2,3},{3,2},{4,5},{5,4},{6,7},{7,6},{8,9},{9,8},{10,11... | collective-permute-start | bytes 110600 | tf_op jit(solution)/shard_map/regroup/ppermute | solution.py:482

commit v3 on v0

--- a/solution.py
+++ b/solution.py
@@ -162,33 +162,36 @@
     sending = pltpu.make_async_copy(pieces_ref, pieces_hbm, sems.at[0])
     sending.start()
 
-    result = filtered(
-        jnp.concatenate(
-            [raw_ref[:, CHUNK * j : CHUNK * (j + 1)] for j in range(chunks)], axis=0
+    @pl.when(lax.axis_index("blk") >= 0)
+    def _():
+        result = filtered(
+            jnp.concatenate(
+                [raw_ref[:, CHUNK * j : CHUNK * (j + 1)] for j in range(chunks)], axis=0
+            )
         )
-    )
-    part = [result[rows * j : rows * (j + 1)] for j in range(chunks)]
-    is_main = lax.broadcasted_iota(jnp.int32, (rows, LANES), 1) < LANES // 2
-    values = []
-    for first in range(0, chunks, per_tile):
-        total = jnp.where(is_main, part[first], 0.0)
-        for step in range(1, min(per_tile, chunks - first)):
-            total = total + pltpu.roll(part[first + step], CHUNK_OUT * step, 1)
-        if first + per_tile < chunks:
-            total = total + jnp.where(is_main, 0.0, part[first + per_tile])
-        values.append(total)
-    rim = jnp.where(is_main, 0.0, part[0])
-    if paired:
-        packed = rim[:SUBLANES]
-        for at in range(1, rows // SUBLANES):
-            group = rim[SUBLANES * at : SUBLANES * (at + 1)]
-            packed = packed + pltpu.roll(group, LANES - EDGE * at, 1)
-        for at, value in enumerate(values):
-            out_ref[rows * at : rows * (at + 1), :] = value
-        out_ref[rows * tiles :, :] = packed
-    else:
-        for at, value in enumerate(values + [rim]):
-            out_ref[:, LANES * at : LANES * (at + 1)] = value
+        part = [result[rows * j : rows * (j + 1)] for j in range(chunks)]
+        is_main = lax.broadcasted_iota(jnp.int32, (rows, LANES), 1) < LANES // 2
+        values = []
+        for first in range(0, chunks, per_tile):
+            total = jnp.where(is_main, part[first], 0.0)
+            for step in range(1, min(per_tile, chunks - first)):
+                total = total + pltpu.roll(part[first + step], CHUNK_OUT * step, 1)
+            if first + per_tile < chunks:
+                total = total + jnp.where(is_main, 0.0, part[first + per_tile])
+            values.append(total)
+        rim = jnp.where(is_main, 0.0, part[0])
+        if paired:
+            packed = rim[:SUBLANES]
+            for at in range(1, rows // SUBLANES):
+                group = rim[SUBLANES * at : SUBLANES * (at + 1)]
+                packed = packed + pltpu.roll(group, LANES - EDGE * at, 1)
+            for at, value in enumerate(values):
+                out_ref[rows * at : rows * (at + 1), :] = value
+            out_ref[rows * tiles :, :] = packed
+        else:
+            for at, value in enumerate(values + [rim]):
+                out_ref[:, LANES * at : LANES * (at + 1)] = value
+
     sending.wait()
 
 

time: 18.9 us -> 18.8 us (level)
  no operation moved by 1% of the time
where the time goes in v3:
time: 18.8 us; the launch traced here: 18.6 us
  starting transfers between devices  9.14 us (49%)
  Pallas kernels  6.34 us (34%)
  waiting for transfers between devices  3.09 us (16%)
    all_to_all x1, starting transfers between devices, local(): lax.all_to_all(pieces.reshape(device_count, 1, main + LANES), ('blk', 'sr...  7.3 us
    all_to_all x1, waiting for transfers between devices, local(): lax.all_to_all(pieces.reshape(device_count, 1, main + LANES), ('blk', 'sr...  2.45 us
    pallas_call x1, Pallas kernels, local(): pl.pallas_call(lambda *refs: decimate_kernel(paired, *refs), out_shape=(s...  2.19 us
    pallas_call x1, Pallas kernels, local(): pl.pallas_call(lambda *refs: correlate_kernel(slots, *refs), out_shape=sh...  1.95 us
    ppermute x1, starting transfers between devices, local(): other = [lax.ppermute(decimated, 'src', [(0, 1), (1, 0)])]  1.83 us
    pallas_call x1, Pallas kernels, local(): pl.pallas_call(prepare_kernel, out_shape=out_shape, in_specs=[VMEM] + [HB...  1.65 us
    ppermute x1, waiting for transfers between devices, local(): other = [lax.ppermute(decimated, 'src', [(0, 1), (1, 0)])]  0.64 us
    pallas_call x1, Pallas kernels, local(): pl.pallas_call(spectra_kernel, out_shape=shaped(rows, NFFT), in_specs=[VM...  0.54 us
  transfers between devices with their start and end apart: 2, of which 2 were waited for; matrix products, arithmetic and copies ran while one was open for 0% of the time, Pallas kernels for 12%

profile of v3, /device:TPU:0, one launch (start us, length us, event | category | flops | bytes accessed | tf_op | source)
XLA Modules:
  0.0 18.6 jit_solution(16699601292488455877)
XLA Ops:
  0.0 2.2 %decimate.1 = (f32[72,128]{1,0:T(8,128)S(1)}, f32[160,128]{1,0:T(8,128)}) custom-call(f32[32,5120]{1,0:T(8,128)} %refs_0_.1, f32[1,64]{1,0:T(1,128)} %bitcast.5, s32[1,32]{1,0:T(1,128)} %bitcast.3, s32[1,2]{1,0:T(1,128)} %picks_hbm.1), custom_call_target="tpu_custom_call" | custom-call | tf_op jit(solution)/shard_map/decimate/pallas_call | solution.py:395
  2.2 7.3 %all-to-all-start = ((f32[32,1,640]{2,1,0:T(1,128)}), f32[32,1,640]{2,1,0:T(1,128)S(1)}, u32[]{:S(2)}, u32[]{:S(2)}) async-start(f32[32,1,640]{2,1,0:T(1,128)} %bitcast.2), calls=%async_computation | async-start | bytes 163840 | tf_op jit(solution)/shard_map/gather_sources/all_to_all | solution.py:423
  9.5 1.8 %collective-permute-start = (f32[72,128]{1,0:T(8,128)S(1)}, f32[72,128]{1,0:T(8,128)S(1)}, u32[]{:S(2)}, u32[]{:S(2)}) collective-permute-start(f32[72,128]{1,0:T(8,128)S(1)} %get-tuple-element.13._.series_ref), channel_id=1, source_target_pairs={{0,1},{1,0},{2,3},{3,2},{4,5},{5,4},{6,7},{7,6},{8,9},{9,8},{10,11... | collective-permute-start | bytes 110600 | tf_op jit(solution)/shard_map/regroup/ppermute | solution.py:483
  11.3 1.7 %prepare.1 = (bf16[256,1024]{1,0:T(8,128)(2,1)S(1)}, bf16[256,1024]{1,0:T(8,128)(2,1)S(1)}, bf16[384,128]{1,0:T(8,128)(2,1)S(1)}, bf16[1024,512]{1,0:T(8,128)(2,...) custom-call(f32[72,128]{1,0:T(8,128)S(1)} %get-tuple-element.13._.series_ref, s32[1,32]{1,0:T(1,128)} %bitcast.4, ...), custom_call_target="tpu_custom_call" | custom-call | bytes 2097152 | tf_op jit(solution)/shard_map/prepare/pallas_call | solution.py:454
  13.0 0.6 %collective-permute-done.refs_0_ = f32[72,128]{1,0:T(8,128)S(1)} collective-permute-done((f32[72,128]{1,0:T(8,128)S(1)}, f32[72,128]{1,0:T(8,128)S(1)}, u32[]{:S(2)}, u32[]{:S(2)}) %collective-permute-start) | collective-permute-done | bytes 36896 | tf_op jit(solution)/shard_map/regroup/ppermute | solution.py:483
  13.6 0.5 %spectra.1.refs_0_ = f32[32,1024]{1,0:T(8,128)S(1)} custom-call(f32[72,128]{1,0:T(8,128)S(1)} %get-tuple-element.13._.series_ref, bf16[256,1024]{1,0:T(8,128)(2,1)S(1)} %get-tuple-element.14.hi_ref.refs_3_, bf16[256,1024]{1,0:T(8,128)(2,1)S(1)} %get-tuple-element.15.lo_ref.refs_4_, bf16[384,128]{1,0:T(8,128)(2,1)S(1)} %get-tuple-element.16.band_ref.refs_5_, ...), custom_call_target="tpu_custom_call" | custom-call | tf_op jit(solution)/shard_map/spectra/pallas_call | solution.py:490
  14.2 2.4 %all-to-all-done.refs_1_ = f32[32,1,640]{2,1,0:T(1,128)S(1)} async-done(((f32[32,1,640]{2,1,0:T(1,128)}), f32[32,1,640]{2,1,0:T(1,128)S(1)}, u32[]{:S(2)}, u32[]{:S(2)}) %all-to-all-start) | async-done | bytes 81952 | tf_op jit(solution)/shard_map/gather_sources/all_to_all | solution.py:423
  16.6 1.9 %correlate.1 = bf16[16,32,512]{2,1,0:T(8,128)(2,1)} custom-call(f32[32,1024]{1,0:T(8,128)S(1)} %spectra.1.refs_0_, f32[32,1,640]{2,1,0:T(1,128)S(1)} %all-to-all-done.refs_1_, f32[2,32,128]{2,1,0:T(8,128)S(1)} %get-tuple-element.19.refs_2_, bf16[256,1024]{1,0:T(8,128)(2,1)S(1)} %get-tuple-element.14.hi_ref.refs_3_, ...), custom_call_target="tpu_custom_call" | custom-call | tf_op jit(solution)/shard_map/correlate/pallas_call | solution.py:500
Async XLA Ops:
  2.2 14.4 %all-to-all-start = ((f32[32,1,640]{2,1,0:T(1,128)}), f32[32,1,640]{2,1,0:T(1,128)S(1)}, u32[]{:S(2)}, u32[]{:S(2)}) async-start(f32[32,1,640]{2,1,0:T(1,128)} %bitcast.2), calls=%async_computation | async-start | bytes 163840 | tf_op jit(solution)/shard_map/gather_sources/all_to_all | solution.py:423
  9.5 4.1 %collective-permute-start = (f32[72,128]{1,0:T(8,128)S(1)}, f32[72,128]{1,0:T(8,128)S(1)}, u32[]{:S(2)}, u32[]{:S(2)}) collective-permute-start(f32[72,128]{1,0:T(8,128)S(1)} %get-tuple-element.13._.series_ref), channel_id=1, source_target_pairs={{0,1},{1,0},{2,3},{3,2},{4,5},{5,4},{6,7},{7,6},{8,9},{9,8},{10,11... | collective-permute-start | bytes 110600 | tf_op jit(solution)/shard_map/regroup/ppermute | solution.py:483
